TPU v7x, 128 devices: a whole 4x4x4 slice. The times are simulated.
128 devices in a mesh: blk: 16 (over x_lo, y, core), node: 8 (over x_hi, z).
Axes of the slice: x: 4 (x_hi: 2, x_lo: 2; x = x_hi * 2 + x_lo), y: 4, z: 4, core: 2. Of those that a mesh axis runs over, the one named last changes fastest.
Arguments:
- images: bfloat16 [49152, 1280], P(('blk', 'node')), may hold values from -11 to 11
- texts: bfloat16 [49152, 1280], P(('blk', 'node')), may hold values from -0.4 to 0.4
- rest_row: float32 [49152], P(('blk', 'node')), may hold values from 2 to 20
- rest_col: float32 [49152], P(('blk', 'node')), may hold values from 2 to 20
Outputs:
- image_grad: float32 [49152, 1280], P(('blk', 'node'))
- text_grad: float32 [49152, 1280], P(('blk', 'node'))
- loss: float32 [], replicated
All inputs are finite; a program needn't handle non-finite values.
Results may differ from a plain program's by a relative error of at most 0.00105.
The roundings to bfloat16 on the way count: a program that leaves them out, or rounds other values in their place, can miss the bound.
Values may be sent and summed in bfloat16 or wider, within the bound.
A program may use at most 192 MiB of HBM per device.

v0:
```python
import jax
import jax.numpy as jnp
from jax import lax
from jax.sharding import PartitionSpec as P

logit_scale = 100.0


def passed_along(value, axis, steps):
    count = lax.axis_size(axis)
    pairs = [(source, (source + steps) % count) for source in range(count)]
    return lax.ppermute(value, axis, pairs)


def combined_all(value, axis, combine):
    everything = jax.tree.map(lambda part: lax.all_gather(part, axis), value)
    leading = jax.tree.map(lambda part: part[0], everything)

    def hop(k, so_far):
        return combine(so_far, jax.tree.map(lambda part: part[k], everything))

    return lax.fori_loop(1, lax.axis_size(axis), hop, leading)


def merge_pair(first, second):
    top = jnp.maximum(first[0], second[0])
    return (top, first[1] * jnp.exp(first[0] - top) + second[1] * jnp.exp(second[0] - top))


def shards(images, texts, rest_row, rest_col):
    rows = images.shape[0]
    nodes = lax.axis_size("node")
    group = nodes * rows
    start = lax.axis_index("node") * rows
    own_block = lax.all_gather(texts, "node", axis=0, tiled=True)
    prev_block = passed_along(own_block, "blk", 1)
    window = jnp.concatenate([prev_block, own_block], 0)
    logits = logit_scale * lax.dot_general(
        images, window, (((1,), (1,)), ((), ())), preferred_element_type=jnp.float32
    )
    row_lse = jnp.logaddexp(rest_row, jax.nn.logsumexp(logits, axis=1))
    col_max = jnp.max(logits, axis=0)
    col_sum = jnp.sum(jnp.exp(logits - col_max[None, :]), axis=0)
    col_max, col_sum = combined_all((col_max, col_sum), "node", merge_pair)
    back_max, back_sum = passed_along((col_max[:group], col_sum[:group]), "blk", -1)
    own_max, own_sum = merge_pair((col_max[group:], col_sum[group:]), (back_max, back_sum))
    mine_max = lax.dynamic_slice_in_dim(own_max, start, rows)
    mine_sum = lax.dynamic_slice_in_dim(own_sum, start, rows)
    col_mine = jnp.logaddexp(rest_col, mine_max + jnp.log(mine_sum))
    prev_mine = passed_along(col_mine, "blk", 1)
    prev_col, own_col = (
        lax.all_gather(prev_mine, "node", axis=0, tiled=True),
        lax.all_gather(col_mine, "node", axis=0, tiled=True),
    )
    col_window = jnp.concatenate([prev_col, own_col], 0)
    diag = jnp.diagonal(lax.dynamic_slice_in_dim(logits, group + start, rows, 1))
    local_terms = jnp.sum(row_lse) + jnp.sum(col_mine) - 2.0 * jnp.sum(diag)
    total_rows = group * lax.axis_size("blk")
    loss = lax.psum(local_terms, ("blk", "node")) / (2.0 * total_rows)
    columns = lax.broadcasted_iota(jnp.int32, logits.shape, 1)
    row_index = lax.broadcasted_iota(jnp.int32, logits.shape, 0)
    marks = jnp.where(columns == group + start + row_index, 2.0, 0.0)
    weights = jnp.exp(logits - row_lse[:, None]) + jnp.exp(logits - col_window[None, :]) - marks
    weights = weights.astype(jnp.bfloat16)
    image_grad = logit_scale * jnp.dot(weights, window, preferred_element_type=jnp.float32)

    def column_slab(first, count):
        picked = lax.dynamic_slice_in_dim(weights, first, count, 1)
        return logit_scale * lax.dot_general(
            picked, images, (((0,), (0,)), ((), ())), preferred_element_type=jnp.float32
        )

    prev_terms = column_slab(0, group)
    arrived = passed_along(prev_terms, "blk", -1)
    text_grad = lax.psum_scatter(
        column_slab(group + jnp.int32(0), lax.axis_size("node") * rows) + arrived,
        "node",
        scatter_dimension=0,
        tiled=True,
    )
    return (image_grad, text_grad, loss)


def solution(mesh):
    return jax.shard_map(
        shards,
        mesh=mesh,
        in_specs=(
            P(("blk", "node"), None),
            P(("blk", "node"), None),
            P(("blk", "node")),
            P(("blk", "node")),
        ),
        out_specs=(P(("blk", "node"), None), P(("blk", "node"), None), P()),
        check_vma=False,
    )
```

profile of v0, /device:TPU:25, one launch (start us, length us, event | category | flops | bytes accessed | tf_op | source)
XLA Modules:
  0.0 749.7 jit_solution(13142284481661398448)
XLA Ops:
  8.0 106.6 %all-gather.6.cloned.1.call-done = bf16[3072,1280]{1,0:T(8,128)(2,1)} async-done(((bf16[384,1280]{1,0:T(8,128)(2,1)}), bf16[3072,1280]{1,0:T(8,128)(2,1)}) %all-gather.6.cloned.1.call-update) | async-done | bytes 7864336 | tf_op jit(solution)/shard_map/all_gather | solution.py:35
  114.6 1.2 collective-permute-start
  115.8 85.1 %collective-permute-done = bf16[3072,1280]{1,0:T(8,128)(2,1)} collective-permute-done((bf16[3072,1280]{1,0:T(8,128)(2,1)}, bf16[3072,1280]{1,0:T(8,128)(2,1)}, u32[]{:S(2)}, u32[]{:S(2)}) %collective-permute-start) | collective-permute-done | bytes 7864352 | tf_op jit(solution)/shard_map/ppermute | solution.py:12
  200.9 6.8 constant_dynamic-update-slice_fusion.1
  207.7 3.7 constant_dynamic-update-slice_fusion
  211.4 14.0 %fusion.8 = (f32[384]{0:T(512)S(1)}, f32[6144]{0:T(1024)S(1)}, f32[6144,384]{1,0:T(8,128)}) fusion(bf16[6144,1280]{1,0:T(8,128)(2,1)} %constant_dynamic-update-slice_fusion, bf16[384,1280]{1,0:T(8,128)(2,1)S(1)} %copy-done), kind=kOutput, calls=%fused_computation.35 | convolution fusion | flops 6046868992 | bytes 26174976 | tf_op jit(solution)/shard_map/dot_general | solution.py:38
  225.4 28.3 %all-gather = f32[49152]{0:T(1024)S(1)} all-gather(f32[6144]{0:T(1024)S(1)} %get-tuple-element.141), channel_id=2, replica_groups=mesh['blk'=16,'node'=8] {'node'}, dimensions={0}, use_global_device_ids=true | all-gather | bytes 221184 | tf_op jit(solution)/shard_map/all_gather | solution.py:16
  253.8 6.9 exponential_reduce_fusion.1
  260.8 27.9 %all-gather.1 = f32[49152]{0:T(1024)S(1)} all-gather(f32[6144]{0:T(1024)S(1)} %get-tuple-element.139), channel_id=3, replica_groups=mesh['blk'=16,'node'=8] {'node'}, dimensions={0}, use_global_device_ids=true | all-gather | bytes 221184 | tf_op jit(solution)/shard_map/all_gather | solution.py:16
  289.5 14.9 %collective-permute-start.1 = (f32[3072]{0:T(1024)S(1)}, f32[3072]{0:T(1024)S(1)}, u32[]{:S(2)}, u32[]{:S(2)}) collective-permute-start(f32[3072]{0:T(1024)S(1)} %slice.21), channel_id=1, source_target_pairs={{0,120},{8,0},{16,8},{24,16},{32,24},{40,32},{48,40},{56,48},{64,5... | collective-permute-start | bytes 36872 | tf_op jit(solution)/shard_map/ppermute | solution.py:12
  305.1 2.9 collective-permute-done.1
  308.0 1.6 collective-permute-done.2
  310.4 25.0 %all-gather.3 = f32[8,1,384]{2,1,0:T(1,128)S(1)} all-gather(f32[1,1,384]{2,1,0:T(1,128)S(1)} %reshape.27), channel_id=1, replica_groups=mesh['blk'=16,'node'=8] {'node'}, dimensions={0}, use_global_device_ids=true | all-gather | bytes 13824 | tf_op jit(solution)/shard_map/all_gather | solution.py:53
  335.3 25.2 %all-gather.2 = f32[8,1,384]{2,1,0:T(1,128)S(1)} all-gather(f32[1,1,384]{2,1,0:T(1,128)S(1)} %reshape.25), channel_id=1, replica_groups=mesh['blk'=16,'node'=8] {'node'}, dimensions={0}, use_global_device_ids=true | all-gather | bytes 13824 | tf_op jit(solution)/shard_map/all_gather | solution.py:52
  360.5 6.1 fusion
  366.6 7.7 %convolution_multiply_fusion = f32[3072,1280]{1,0:T(8,128)} fusion(bf16[384,1280]{1,0:T(8,128)(2,1)S(1)} %copy-done, bf16[384,6144]{0,1:T(8,128)(2,1)S(1)} %fusion), kind=kOutput, calls=%fused_computation.5 | convolution fusion | flops 3023831040 | bytes 19070976 | tf_op jit(solution)/shard_map/dot_general | solution.py:69
  374.3 9.7 %collective-permute-start.4 = (f32[3072,1280]{1,0:T(8,128)}, f32[3072,1280]{1,0:T(8,128)S(1)}, u32[]{:S(2)}, u32[]{:S(2)}) collective-permute-start(f32[3072,1280]{1,0:T(8,128)} %convolution_multiply_fusion), channel_id=1, source_target_pairs={{0,120},{8,0},{16,8},{24,16},{32,24},{40,32},{48,40},{56,48},{64,5... | collective-permute-start | bytes 47185928 | tf_op jit(solution)/shard_map/ppermute | solution.py:12
  384.0 170.1 %collective-permute-done.4 = f32[3072,1280]{1,0:T(8,128)S(1)} collective-permute-done((f32[3072,1280]{1,0:T(8,128)}, f32[3072,1280]{1,0:T(8,128)S(1)}, u32[]{:S(2)}, u32[]{:S(2)}) %collective-permute-start.4) | collective-permute-done | bytes 15728672 | tf_op jit(solution)/shard_map/ppermute | solution.py:12
  554.1 10.2 %multiply_add_fusion.1 = f32[3072,1280]{1,0:T(8,128)} fusion(f32[3072,1280]{1,0:T(8,128)S(1)} %collective-permute-done.4, bf16[384,1280]{1,0:T(8,128)(2,1)S(1)} %copy-done, bf16[384,6144]{0,1:T(8,128)(2,1)} %copy-done.1), kind=kOutput, calls=%fused_computation.4 | convolution fusion | flops 3027763200 | bytes 34799616 | tf_op jit(solution)/shard_map/dot_general | solution.py:69
  564.3 1.1 dynamic-slice_bitcast_fusion
  565.4 3.5 gather_fusion
  571.6 85.3 %psum.7 = f32[]{:T(128)} all-reduce(f32[]{:T(128)S(6)} %sub.87), channel_id=1, replica_groups=mesh['blk'=16,'node'=8] {'blk','node'}, use_global_device_ids=true, to_apply=%region_10.11 | all-reduce | flops 1 | bytes 8 | tf_op jit(solution)/shard_map/psum | solution.py:59
  657.5 12.5 %convolution_multiply_fusion.2 = f32[384,1280]{1,0:T(8,128)} fusion(bf16[384,6144]{0,1:T(8,128)(2,1)} %copy-done.1, bf16[6144,1280]{1,0:T(8,128)(2,1)} %constant_dynamic-update-slice_fusion), kind=kOutput, calls=%fused_computation.12 | convolution fusion | flops 6040289280 | bytes 22413312 | tf_op jit(solution)/shard_map/dot_general | solution.py:65
  670.0 71.7 %reduce-scatter.2.cloned.1.call-done = f32[384,1280]{1,0:T(8,128)} async-done(((f32[3072,1280]{1,0:T(8,128)}), f32[384,1280]{1,0:T(8,128)}) %reduce-scatter.2.cloned.1.call-update) | async-done | bytes 1966096 | tf_op jit(solution)/shard_map/reduce_scatter | solution.py:75
  (51 shorter events, 4.2 us)
Async XLA Ops:
  7.2 204.2 %copy-start = (bf16[384,1280]{1,0:T(8,128)(2,1)S(1)}, bf16[384,1280]{1,0:T(8,128)(2,1)}, u32[]{:S(2)}) copy-start(bf16[384,1280]{1,0:T(8,128)(2,1)} %param.6) | copy-start | bytes 2949124
  7.2 107.4 %all-gather.6.cloned.1.call-start = ((), (), s32[]{:S(2)}) async-start(), calls=%async_computation.1 | async-start | bytes 8847360 | tf_op jit(solution)/shard_map/all_gather | solution.py:35
  7.9 733.8 %reduce-scatter.2.cloned.1.call-start = ((), (), s32[]{:S(2)}) async-start(), calls=%async_computation.2 | async-start | bytes 17694720 | tf_op jit(solution)/shard_map/reduce_scatter | solution.py:75
  114.6 86.3 %collective-permute-start = (bf16[3072,1280]{1,0:T(8,128)(2,1)}, bf16[3072,1280]{1,0:T(8,128)(2,1)}, u32[]{:S(2)}, u32[]{:S(2)}) collective-permute-start(bf16[3072,1280]{1,0:T(8,128)(2,1)} %all-gather.6.cloned.1.call-done), channel_id=1, source_target_pairs={{0,8},{8,16},{16,24},{24,32},{32,40},{40,48},{48,56},{56,64},{64,7... | collective-permute-start | bytes 23592968 | tf_op jit(solution)/shard_map/ppermute | solution.py:12
  115.8 91.9 %slice-start = ((s8[7864320]{0:T(1024)(128)(4,1)}), s8[4194304]{0:T(1024)(128)(4,1)S(1)}, s32[]{:S(2)}) async-start(s8[7864320]{0:T(1024)(128)(4,1)} %bitcast.20), calls=%async_computation.3 | async-start | bytes 8388608
  115.8 91.9 %slice-start.1 = ((s8[7864320]{0:T(1024)(128)(4,1)}), s8[3670016]{0:T(1024)(128)(4,1)S(1)}, s32[]{:S(2)}) async-start(s8[7864320]{0:T(1024)(128)(4,1)} %bitcast.20), calls=%async_computation.4 | async-start | bytes 7340032
  225.4 79.0 %copy-start.2 = (f32[384]{0:T(512)S(1)}, f32[384]{0:T(512)}, u32[]{:S(2)}) copy-start(f32[384]{0:T(512)} %param.8) | copy-start | bytes 4612
  225.4 84.2 %copy-start.3 = (f32[384]{0:T(512)S(1)}, f32[384]{0:T(512)}, u32[]{:S(2)}) copy-start(f32[384]{0:T(512)} %param.9) | copy-start | bytes 4612
  289.5 18.5 %collective-permute-start.1 = (f32[3072]{0:T(1024)S(1)}, f32[3072]{0:T(1024)S(1)}, u32[]{:S(2)}, u32[]{:S(2)}) collective-permute-start(f32[3072]{0:T(1024)S(1)} %slice.21), channel_id=1, source_target_pairs={{0,120},{8,0},{16,8},{24,16},{32,24},{40,32},{48,40},{56,48},{64,5... | collective-permute-start | bytes 36872 | tf_op jit(solution)/shard_map/ppermute | solution.py:12
  304.4 5.2 collective-permute-start.2
  310.3 25.0 %collective-permute-start.3 = (f32[384]{0:T(512)S(1)}, f32[384]{0:T(512)S(1)}, u32[]{:S(2)}, u32[]{:S(2)}) collective-permute-start(f32[384]{0:T(512)S(1)} %get-tuple-element.155), channel_id=1, source_target_pairs={{0,8},{8,16},{16,24},{24,32},{32,40},{40,48},{48,56},{56,64},{64,7... | collective-permute-start | bytes 4616 | tf_op jit(solution)/shard_map/ppermute | solution.py:12
  366.6 7.7 %copy-start.1 = (bf16[384,6144]{0,1:T(8,128)(2,1)}, bf16[384,6144]{0,1:T(8,128)(2,1)S(1)}, u32[]{:S(2)}) copy-start(bf16[384,6144]{0,1:T(8,128)(2,1)S(1)} %fusion) | copy-start | bytes 14155780
  374.3 179.8 %collective-permute-start.4 = (f32[3072,1280]{1,0:T(8,128)}, f32[3072,1280]{1,0:T(8,128)S(1)}, u32[]{:S(2)}, u32[]{:S(2)}) collective-permute-start(f32[3072,1280]{1,0:T(8,128)} %convolution_multiply_fusion), channel_id=1, source_target_pairs={{0,120},{8,0},{16,8},{24,16},{32,24},{40,32},{48,40},{56,48},{64,5... | collective-permute-start | bytes 47185928 | tf_op jit(solution)/shard_map/ppermute | solution.py:12
Sparse Core Ops, SparseCore 0:
  10.3 104.2 all-gather.5
  564.4 177.2 reduce-scatter.1
where the time goes:
time: 751 us; the launch traced here: 750 us
  waiting for transfers between devices  439 us (58%)
  blocking collectives  192 us (26%)
  matrix products  44.4 us (6%)
  starting transfers between devices  26 us (3%)
  between operations  17.9 us (2%)
  local copies, waits for them, and re-layouts  15.5 us (2%)
  other arithmetic  15.3 us (2%)
    ppermute x5, waiting for transfers between devices, passed_along(): return lax.ppermute(value, axis, pairs)  260 us
    all_gather x1, waiting for transfers between devices, shards(): own_block = lax.all_gather(texts, 'node', axis=0, tiled=True)  107 us
    psum x1, blocking collectives, shards(): loss = lax.psum(local_terms, ('blk', 'node')) / (2.0 * total_rows)  85.3 us
    reduce_scatter x1, waiting for transfers between devices, shards(): lax.psum_scatter(column_slab(group + jnp.int32(0), lax.axis_size('node')...  71.7 us
    all_gather x2, blocking collectives, combined_all(): everything = jax.tree.map(lambda part: lax.all_gather(part, axis), value)  56.2 us
    ppermute x5, starting transfers between devices, passed_along(): return lax.ppermute(value, axis, pairs)  25.9 us
    all_gather x1, blocking collectives, shards(): lax.all_gather(prev_mine, 'node', axis=0, tiled=True)  25.2 us
    all_gather x1, blocking collectives, shards(): lax.all_gather(col_mine, 'node', axis=0, tiled=True)  25 us
  transfers between devices with their start and end apart: 7, of which 6 were waited for; matrix products, arithmetic and copies ran while one was open for 2% of the time, Pallas kernels for 0%

commit v1 on v0

v1 whole, which is shorter than its diff:
```python
import functools

import jax
import jax.numpy as jnp
from jax import lax
from jax.experimental import pallas as pl
from jax.experimental.pallas import tpu as pltpu
from jax.sharding import PartitionSpec as P


MESH = pl.DeviceIdType.MESH
F32, BF16 = jnp.float32, jnp.bfloat16
logit_scale = 100.0
LANES = 128
CHUNK = 16
PAD = 16
WIDE = 256
POWER_RANGE = 2.0**18

(IMG_R0, IMG_R1, IMG_L1, IMG_L0, FWD_R, FWD_L, TXT_X0, TXT_X1, TXT_N0, TXT_N1, FWD_N0, FWD_N1) = range(12)
(ROW_R, ROW_L, ROW_F, OWN_X, OWN_NS, OWN_NO, PRV_X, PRV_PS, PRV_PO) = range(12, 21)
OUT = 21
(F_R, F_L, R_DIR, L_DIR, R_ACC, L_ACC, Y_0, Y_1, Y_2, Y_3, X_0, X_1) = range(12)
UNITS = 12
SUM = OUT + UNITS


def kernel(
    n_blk, img_ref, txt_ref, rr_ref, rc_ref, ig_ref, tg_ref, loss_ref,
    im, tx, s_ref, w, wt, rowp, colm, cols, rstat, rl, co, cp, cl, keep, snd, rcv, lsnd, lrcv,
    ss, rs, lsem,
):
    rows, width = img_ref.shape
    half = rows // 2
    tile = 4 * rows
    b = lax.axis_index("blk")
    node = lax.axis_index("node")
    i, z = node // 4, node % 4
    zr, zl, zf = (z + 1) % 4, (z + 3) % 4, (z + 2) % 4
    nxt, prv = (b + 1) % n_blk, (b + n_blk - 1) % n_blk
    oi = 1 - i

    def dev(blk, hi, zz):
        return (blk, hi * 4 + zz)

    right, left, far = dev(b, i, zr), dev(b, i, zl), dev(b, i, zf)
    across = dev(b, oi, z)
    n_same, n_other, p_same, p_other = dev(nxt, i, z), dev(nxt, oi, z), dev(prv, i, z), dev(prv, oi, z)

    def flip(value, step):
        return value + step - 2 * step * ((value // step) % 2)

    steps, step = [], 1
    while step < n_blk:
        steps.append(step)
        step *= 2
    flips = [dev(b, i, flip(z, 1)), far, across] + [dev(flip(b, step), i, z) for step in steps]

    load_img = pltpu.make_async_copy(img_ref, im.at[pl.ds(pl.multiple_of(z * rows, rows), rows)], lsem.at[0])
    load_txt = pltpu.make_async_copy(txt_ref, tx.at[pl.ds(pl.multiple_of(i * rows, rows), rows)], lsem.at[1])
    load_img.start()
    load_txt.start()

    barrier = pltpu.get_barrier_semaphore()
    partners = [right, left, far, across, n_same, n_other, p_same, p_other]
    partners += [dev(flip(b, step), i, z) for step in steps[1:]]
    for partner in partners:
        pl.semaphore_signal(barrier, inc=1, device_id=partner, device_id_type=MESH)
    pl.semaphore_wait(barrier, len(partners))
    load_img.wait()
    load_txt.wait()

    def remote(k, src, dst, target):
        return pltpu.make_async_remote_copy(
            src_ref=src, dst_ref=dst, send_sem=ss.at[k], recv_sem=rs.at[k], device_id=target, device_id_type=MESH
        )

    def block(slot):
        return pl.ds(pl.multiple_of(slot * rows, rows), rows)

    def part(slot, h):
        return pl.ds(pl.multiple_of(slot * rows + h * half, half), half)

    copies = {}

    def send(k, src, dst, target):
        copies[k] = remote(k, src, dst, target)
        copies[k].start()

    def same(k, ref, where, target):
        send(k, ref.at[where], ref.at[where], target)

    same(IMG_R0, im, part(z, 0), right)
    same(IMG_L1, im, part(z, 1), left)
    same(TXT_X0, tx, part(i, 0), across)
    send(TXT_N0, tx.at[part(i, 0)], tx.at[part(2 + i, 0)], n_same)
    same(IMG_R1, im, part(z, 1), right)
    same(IMG_L0, im, part(z, 0), left)
    same(TXT_X1, tx, part(i, 1), across)
    send(TXT_N1, tx.at[part(i, 1)], tx.at[part(2 + i, 1)], n_same)
    copies[IMG_R0].wait_recv()
    same(FWD_R, im, part(zl, 0), right)
    copies[IMG_L1].wait_recv()
    same(FWD_L, im, part(zr, 1), left)
    copies[TXT_X0].wait_recv()
    send(FWD_N0, tx.at[part(oi, 0)], tx.at[part(2 + oi, 0)], n_same)
    copies[TXT_X1].wait_recv()
    send(FWD_N1, tx.at[part(oi, 1)], tx.at[part(2 + oi, 1)], n_same)
    for k in (TXT_N0, TXT_N1, FWD_N0, FWD_N1):
        copies[k].wait_recv()

    n_chunks = rows // CHUNK
    n_lane = tile // LANES
    lanes = lambda k: pl.ds(k * LANES, LANES)

    def logits_block(q, order):
        base = pl.multiple_of(q * rows, rows)

        @pl.loop(0, 4)
        def _(c):
            span = pl.ds(pl.multiple_of(c * rows, rows), rows)
            s_ref[block(q), span] = logit_scale * lax.dot_general(
                im[block(q), :], tx[span, :], (((1,), (1,)), ((), ())), preferred_element_type=F32
            )

        def chunk(r):
            return pl.ds(pl.multiple_of(base + r * CHUNK, CHUNK), CHUNK)

        def row_pass(r, top):
            s = s_ref[chunk(r), :]
            m = jnp.max(s, axis=1, keepdims=True)
            total = jnp.sum(jnp.exp(s - m), axis=1, keepdims=True)
            rowp[chunk(r), :] = jnp.broadcast_to(m + jnp.log(total), (CHUNK, LANES))
            return jnp.maximum(top, jnp.maximum(s[:8], s[8:]))

        top = lax.fori_loop(0, n_chunks, row_pass, jnp.full((8, tile), -jnp.inf, F32))
        top = jnp.broadcast_to(jnp.max(top, axis=0, keepdims=True), (8, tile))

        def col_pass(r, total):
            s = s_ref[chunk(r), :]
            return total + jnp.exp(s[:8] - top) + jnp.exp(s[8:] - top)

        total = lax.fori_loop(0, n_chunks, col_pass, jnp.zeros((8, tile), F32))
        colm[pl.ds(order * 8, 8), :] = top
        cols[pl.ds(order * 8, 8), :] = jnp.broadcast_to(jnp.sum(total, axis=0, keepdims=True), (8, tile))
        rstat[:, block(q)] = jnp.transpose(rowp[block(q), :])[:8, :]

    logits_block(z, 0)
    copies[IMG_R1].wait_recv()
    logits_block(zl, 1)
    copies[IMG_L0].wait_recv()
    logits_block(zr, 2)
    copies[FWD_R].wait_recv()
    copies[FWD_L].wait_recv()
    logits_block(zf, 3)

    def join(a, c):
        top = jnp.maximum(a, c)
        return top + jnp.log(jnp.exp(a - top) + jnp.exp(c - top))

    rstat[:, block(z)] = join(rstat[:, block(z)], jnp.broadcast_to(rr_ref[...], (8, rows)))
    rl[z] = rstat[...]
    for k, target in ((ROW_R, right), (ROW_L, left), (ROW_F, far)):
        send(k, rstat, rl.at[z], target)
    top = functools.reduce(jnp.maximum, [colm[pl.ds(8 * k, 8), :] for k in range(4)])
    total = functools.reduce(
        jnp.add, [cols[pl.ds(8 * k, 8), :] * jnp.exp(colm[pl.ds(8 * k, 8), :] - top) for k in range(4)]
    )
    both = top + jnp.log(total)
    co[i] = both[:, : 2 * rows]
    cp[2 + i] = both[:, 2 * rows :]
    co[i, :, block(i)] = join(co[i, :, block(i)], jnp.broadcast_to(rc_ref[...], (8, rows)))
    send(OWN_X, co.at[i], co.at[i], across)
    send(OWN_NS, co.at[i], cp.at[i], n_same)
    send(OWN_NO, co.at[i], cp.at[i], n_other)
    send(PRV_X, cp.at[2 + i], cp.at[2 + i], across)
    send(PRV_PS, cp.at[2 + i], co.at[2 + i], p_same)
    send(PRV_PO, cp.at[2 + i], co.at[2 + i], p_other)

    def diag_pass(r, total):
        s = s_ref[pl.ds(pl.multiple_of(z * rows + r * CHUNK, CHUNK), CHUNK), block(i)]
        row = lax.broadcasted_iota(jnp.int32, s.shape, 0) + r * CHUNK
        return total + jnp.where(lax.broadcasted_iota(jnp.int32, s.shape, 1) == row, s, 0.0)

    diag = jnp.sum(lax.fori_loop(0, n_chunks, diag_pass, jnp.zeros((CHUNK, rows), F32)), keepdims=True)

    def merged(parts):
        top = functools.reduce(jnp.maximum, parts)
        return top + jnp.log(functools.reduce(jnp.add, [jnp.exp(p - top) for p in parts]))

    for k in range(ROW_R, PRV_PO + 1):
        copies[k].wait_recv()
    cl[:, : 2 * rows] = merged([co[k] for k in range(4)])
    cl[:, 2 * rows :] = merged([cp[k] for k in range(4)])
    rstat2 = merged([rl[k] for k in range(4)])
    for q in range(4):
        column = jnp.broadcast_to(rstat2[0:1, q * rows : (q + 1) * rows], (LANES, rows))
        rowp[pl.ds(q * rows, rows), :] = jnp.transpose(column)

    terms = (
        jnp.sum(rowp[block(z), 0:1], keepdims=True)
        + jnp.sum(cl[0:1, block(i)], keepdims=True)
        - 2.0 * diag
    )
    loss_ref[...] = jnp.broadcast_to(terms, loss_ref.shape)

    def loss_send(k):
        lsnd[k] = loss_ref[...]
        send(SUM + k, lsnd.at[k], lrcv.at[k], flips[k])

    def loss_next(k):
        copies[SUM + k].wait_recv()
        loss_ref[...] = lsnd[k] + lrcv[k]

    def weights_block(q):
        mine = q == z

        @pl.loop(0, n_chunks)
        def _(r):
            where = pl.ds(pl.multiple_of(q * rows + r * CHUNK, CHUNK), CHUNK)
            row_lse = rowp[where, :]
            row = lax.broadcasted_iota(jnp.int32, (CHUNK, LANES), 0) + (r * CHUNK + i * rows)
            target = jnp.where(mine, row, -1) - lax.broadcasted_iota(jnp.int32, (CHUNK, LANES), 1)
            for k in range(n_lane):
                s = s_ref[where, lanes(k)]
                value = jnp.exp(s - row_lse) + jnp.exp(s - cl[0:1, lanes(k)])
                if k < n_lane // 2:
                    value = value - jnp.where(target == k * LANES, 2.0, 0.0)
                w[where, lanes(k)] = value.astype(BF16)

    def turn_block(q):
        @pl.loop(0, 4)
        def _(t):
            wt[block(t), block(q)] = jnp.transpose(w[block(q), block(t)])

    def product(left_ref, slot, right_ref, span):
        return logit_scale * jnp.dot(left_ref[block(slot), :], right_ref[:, span], preferred_element_type=F32)

    def encode(value, unit, span):
        top = jnp.maximum(jnp.max(jnp.abs(value), axis=0, keepdims=True), 1e-30)
        snd[unit, pl.ds(half, PAD), span] = jnp.broadcast_to(top, (PAD, WIDE)).astype(BF16)
        top = snd[unit, pl.ds(half, PAD), span].astype(F32)[0:1]
        u = value * (POWER_RANGE / top)
        u2 = u * u
        u4 = u2 * u2
        snd[unit, pl.ds(0, half), span] = (u4 * u2 * u).astype(BF16)

    def decode(unit, span):
        code = rcv[unit, pl.ds(0, half), span].astype(F32)
        top = rcv[unit, pl.ds(half, PAD), span].astype(F32)[0:1] * (1.0 / POWER_RANGE)
        size = jnp.abs(code)
        root = jnp.exp2(jnp.log2(size) * (1.0 / 7.0))
        return jnp.where(size > 0.0, jnp.where(code < 0.0, -root, root), 0.0) * top

    def unit_send(unit, target):
        send(OUT + unit, snd.at[unit], rcv.at[unit], target)

    def arrived(unit):
        copies[OUT + unit].wait_recv()

    def columns(body):
        @pl.loop(0, width // WIDE)
        def _(n):
            body(pl.ds(pl.multiple_of(n * WIDE, WIDE), WIDE))

    lo, hi = pl.ds(0, half), pl.ds(half, half)

    weights_block(zf)

    @columns
    def _(span):
        value = product(w, zf, tx, span)
        encode(value[:half], F_R, span)
        encode(value[half:], F_L, span)

    unit_send(F_R, right)
    unit_send(F_L, left)
    loss_send(0)

    weights_block(zr)
    weights_block(zl)
    weights_block(z)
    for q in range(4):
        turn_block(q)

    @columns
    def _(span):
        value = product(wt, 2 + oi, im, span)
        encode(value[:half], Y_0, span)
        encode(value[half:], Y_1, span)

    unit_send(Y_0, p_same)
    unit_send(Y_1, p_same)
    loss_next(0)
    loss_send(1)

    @columns
    def _(span):
        value = product(w, zr, tx, span)
        keep[0, :, span] = value[:half]
        encode(value[half:], R_DIR, span)

    unit_send(R_DIR, right)

    @columns
    def _(span):
        value = product(w, zl, tx, span)
        encode(value[:half], L_DIR, span)
        keep[1, :, span] = value[half:]

    unit_send(L_DIR, left)
    loss_next(1)
    loss_send(2)

    @columns
    def _(span):
        value = product(wt, 2 + i, im, span)
        encode(value[:half], Y_2, span)
        encode(value[half:], Y_3, span)

    unit_send(Y_2, p_same)
    unit_send(Y_3, p_same)

    @columns
    def _(span):
        value = product(wt, oi, im, span)
        keep[2, :, span] = value[:half]
        keep[3, :, span] = value[half:]

    loss_next(2)
    loss_send(3)

    def relay(got, kept, out, target):
        arrived(got)

        @columns
        def _(span):
            encode(keep[kept, :, span] + decode(got, span), out, span)

        unit_send(out, target)

    relay(F_R, 0, R_ACC, right)
    relay(F_L, 1, L_ACC, left)
    relay(Y_0, 2, X_0, across)
    relay(Y_1, 3, X_1, across)

    @columns
    def _(span):
        ig_ref[:, span] = product(w, z, tx, span)

    @columns
    def _(span):
        tg_ref[:, span] = product(wt, i, im, span)

    for k in range(3, len(flips)):
        loss_next(k)
        if k + 1 < len(flips):
            loss_send(k + 1)
    loss_ref[...] = loss_ref[...] / (2.0 * (n_blk * 8 * rows))

    def add(got, ref, where):
        arrived(got)

        @columns
        def _(span):
            ref[where, span] = ref[where, span] + decode(got, span)

    add(Y_2, tg_ref, lo)
    add(Y_3, tg_ref, hi)
    add(R_DIR, ig_ref, hi)
    add(L_DIR, ig_ref, lo)
    add(R_ACC, ig_ref, lo)
    add(L_ACC, ig_ref, hi)
    add(X_0, tg_ref, lo)
    add(X_1, tg_ref, hi)

    for copy in copies.values():
        copy.wait_send()


def shards(n_blk, images, texts, rest_row, rest_col):
    rows, width = images.shape
    tile = 4 * rows
    n_sum = 3 + (n_blk - 1).bit_length()
    vmem = pl.BlockSpec(memory_space=pltpu.VMEM)
    hbm = pl.BlockSpec(memory_space=pl.ANY)
    image_grad, text_grad, loss = pl.pallas_call(
        functools.partial(kernel, n_blk),
        out_shape=(
            jax.ShapeDtypeStruct((rows, width), F32),
            jax.ShapeDtypeStruct((rows, width), F32),
            jax.ShapeDtypeStruct((8, LANES), F32),
        ),
        in_specs=[hbm, hbm, vmem, vmem],
        out_specs=(vmem, vmem, vmem),
        scratch_shapes=[
            pltpu.VMEM((tile, width), BF16),
            pltpu.VMEM((tile, width), BF16),
            pltpu.VMEM((tile, tile), F32),
            pltpu.VMEM((tile, tile), BF16),
            pltpu.VMEM((tile, tile), BF16),
            pltpu.VMEM((tile, LANES), F32),
            pltpu.VMEM((32, tile), F32),
            pltpu.VMEM((32, tile), F32),
            pltpu.VMEM((8, tile), F32),
            pltpu.VMEM((4, 8, tile), F32),
            pltpu.VMEM((4, 8, 2 * rows), F32),
            pltpu.VMEM((4, 8, 2 * rows), F32),
            pltpu.VMEM((8, tile), F32),
            pltpu.VMEM((4, rows // 2, width), F32),
            pltpu.VMEM((UNITS, rows // 2 + PAD, width), BF16),
            pltpu.VMEM((UNITS, rows // 2 + PAD, width), BF16),
            pltpu.VMEM((n_sum, 8, LANES), F32),
            pltpu.VMEM((n_sum, 8, LANES), F32),
            pltpu.SemaphoreType.DMA((SUM + n_sum,)),
            pltpu.SemaphoreType.DMA((SUM + n_sum,)),
            pltpu.SemaphoreType.DMA((2,)),
        ],
        compiler_params=pltpu.CompilerParams(
            collective_id=0, has_side_effects=True, vmem_limit_bytes=60 << 20
        ),
        cost_estimate=pl.CostEstimate(
            flops=6 * tile * tile * width, bytes_accessed=8 * rows * width * 4, transcendentals=4 * tile * tile
        ),
    )(images, texts, rest_row[None, :], rest_col[None, :])
    return image_grad, text_grad, loss[0, 0]


def solution(mesh):
    return jax.shard_map(
        functools.partial(shards, mesh.shape["blk"]),
        mesh=mesh,
        in_specs=(
            P(("blk", "node"), None),
            P(("blk", "node"), None),
            P(("blk", "node")),
            P(("blk", "node")),
        ),
        out_specs=(P(("blk", "node"), None), P(("blk", "node"), None), P()),
        check_vma=False,
    )
```

time: 751 us -> 165 us (0.22)
  the two profiles are of different devices: /device:TPU:25 before, /device:TPU:2 now
where the time goes in v1:
time: 165 us
  Pallas kernels  156 us (95%)
  local copies, waits for them, and re-layouts  8.04 us (5%)
    pallas_call x1, Pallas kernels, shards(): pl.pallas_call(functools.partial(kernel, n_blk), out_shape=(jax.ShapeDtyp...  156 us
    unnamed x4, local copies, waits for them, and re-layouts  4.36 us

profile of v1, /device:TPU:2, one launch (start us, length us, event | category | flops | bytes accessed | tf_op | source)
XLA Modules:
  0.0 165.2 jit_solution(3930835312203802070)
XLA Ops:
  0.6 1.2 broadcast_in_dim.6.rr_ref
  1.9 1.2 broadcast_in_dim.7.rc_ref
  3.1 156.5 %shard_map.67 = (f32[384,1280]{1,0:T(8,128)}, f32[384,1280]{1,0:T(8,128)}, f32[8,128]{1,0:T(8,128)}) custom-call(bf16[384,1280]{1,0:T(8,128)(2,1)} %img_ref.1, bf16[384,1280]{1,0:T(8,128)(2,1)} %txt_ref.1, f32[1,384]{1,0:T(1,128)} %broadcast_in_dim.6.rr_ref, f32[1,384]{1,0:T(1,128)} %broadcast_in_dim.7.rc_ref), custom_call_target="tpu_custom_call" | custom-call | flops 18119393280 | bytes 15728640 | tf_op jit(solution)/shard_map/pallas_call | solution.py:387
  159.6 1.2 slice.3
  160.8 0.0 copy-start
  160.8 3.1 %copy.9 = f32[384,1280]{1,0:T(8,128)} copy(f32[384,1280]{1,0:T(8,128)} %get-tuple-element.12) | data formatting | bytes 3932160
  163.9 0.0 copy-done
  163.9 1.3 copy.10
Async XLA Ops:
  160.8 3.1 %copy-start = (f32[384,1280]{1,0:T(8,128)S(1)}, f32[384,1280]{1,0:T(8,128)}, u32[]{:S(2)}) copy-start(f32[384,1280]{1,0:T(8,128)} %get-tuple-element.13) | copy-start | bytes 5898244

commit v2 on v1

v2 whole, which is shorter than its diff:
```python
import functools

import jax
import jax.numpy as jnp
from jax import lax
from jax.experimental import pallas as pl
from jax.experimental.pallas import tpu as pltpu
from jax.sharding import PartitionSpec as P


MESH = pl.DeviceIdType.MESH
F32, BF16 = jnp.float32, jnp.bfloat16
logit_scale = 100.0
LANES = 128
CHUNK = 16
PAD = 16
WIDE = 256
POWER_RANGE = 2.0**18

(IMG_R0, IMG_R1, IMG_L1, IMG_L0, FWD_R, FWD_L, TXT_X0, TXT_X1, TXT_N0, TXT_N1, FWD_N0, FWD_N1) = range(12)
(ROW_R, ROW_L, ROW_F, OWN_X, OWN_NS, OWN_NO, PRV_X, PRV_PS, PRV_PO) = range(12, 21)
OUT = 21
(F_R, F_L, R_DIR, L_DIR, R_ACC, L_ACC, Y_0, Y_1, Y_2, Y_3, X_0, X_1) = range(12)
UNITS = 12
SUM = OUT + UNITS


def kernel(
    n_blk, img_ref, txt_ref, rr_ref, rc_ref, ig_ref, tg_ref, loss_ref,
    im, tx, s_ref, w, rowp, rows_s, colm, cols, rstat, rl, co, cp, cl, keep, acc, snd, rcv, lacc, lsnd, terms_ref,
    ss, rs, lsem,
):
    rows, width = img_ref.shape
    half = rows // 2
    tile = 4 * rows
    b = lax.axis_index("blk")
    node = lax.axis_index("node")
    i, z = node // 4, node % 4
    zr, zl, zf = (z + 1) % 4, (z + 3) % 4, (z + 2) % 4
    nxt, prv = (b + 1) % n_blk, (b + n_blk - 1) % n_blk
    oi = 1 - i

    def dev(blk, hi, zz):
        return (blk, hi * 4 + zz)

    right, left, far = dev(b, i, zr), dev(b, i, zl), dev(b, i, zf)
    across = dev(b, oi, z)
    n_same, n_other, p_same, p_other = dev(nxt, i, z), dev(nxt, oi, z), dev(prv, i, z), dev(prv, oi, z)

    def flip(value, step):
        return value + step - 2 * step * ((value // step) % 2)

    def flips(value, step, k):
        if k % 2:
            value = flip(value, step)
        return flip(value, 2 * step) if k // 2 else value

    blk_stages, step = [], 1
    while step < n_blk:
        count = min(4, n_blk // step)
        blk_stages.append((step, count))
        step *= count

    load_img = pltpu.make_async_copy(img_ref, im.at[pl.ds(pl.multiple_of(z * rows, rows), rows)], lsem.at[0])
    load_txt = pltpu.make_async_copy(txt_ref, tx.at[pl.ds(pl.multiple_of(i * rows, rows), rows)], lsem.at[1])
    load_img.start()
    load_txt.start()

    barrier = pltpu.get_barrier_semaphore()
    partners = [right, left, far, across, n_same, n_other, p_same, p_other]
    for step, count in blk_stages:
        partners += [dev(flips(b, step, k), i, z) for k in range(1, count) if step * k != 1]
    for partner in partners:
        pl.semaphore_signal(barrier, inc=1, device_id=partner, device_id_type=MESH)
    pl.semaphore_wait(barrier, len(partners))
    load_img.wait()
    load_txt.wait()

    def remote(k, src, dst, target):
        return pltpu.make_async_remote_copy(
            src_ref=src, dst_ref=dst, send_sem=ss.at[k], recv_sem=rs.at[k], device_id=target, device_id_type=MESH
        )

    def block(slot):
        return pl.ds(pl.multiple_of(slot * rows, rows), rows)

    def part(slot, h):
        return pl.ds(pl.multiple_of(slot * rows + h * half, half), half)

    copies = {}

    def send(k, src, dst, target):
        copies[k] = remote(k, src, dst, target)
        copies[k].start()

    def same(k, ref, where, target):
        send(k, ref.at[where], ref.at[where], target)

    odd = b % 2 == 1
    turn = b % 8 == 7

    def start(k, src, dst, target):
        copies[k] = remote(k, src, dst, target)
        return copies[k]

    same(IMG_R0, im, part(z, 0), right)
    same(IMG_L1, im, part(z, 1), left)
    own = [
        start(k, tx.at[part(i, h)], tx.at[part(2 + i, h)], n_same) for h, k in enumerate((TXT_N0, TXT_N1))
    ]

    @pl.when(jnp.logical_not(turn))
    def _():
        own[0].start()
        own[1].start()

    swap = [start(k, tx.at[part(i, h)], tx.at[part(i, h)], across) for h, k in enumerate((TXT_X0, TXT_X1))]

    swap[0].start()
    swap[1].start()

    same(IMG_R1, im, part(z, 1), right)
    same(IMG_L0, im, part(z, 0), left)
    slot = jnp.where(turn, i, oi)
    reach = dev(nxt, jnp.where(turn, oi, i), z)
    fwd = [
        start(k, tx.at[part(slot, h)], tx.at[part(2 + slot, h)], reach) for h, k in enumerate((FWD_N0, FWD_N1))
    ]

    def pick(t, *options):
        value = options[0]
        for k in range(1, len(options)):
            value = jnp.where(t == k, options[k], value)
        return value

    def logits_pair(q, p):
        pair = pl.ds(pl.multiple_of(p * 2 * rows, 2 * rows), 2 * rows)
        s_ref[block(q), pair] = logit_scale * lax.dot_general(
            im[block(q), :], tx[pair, :], (((1,), (1,)), ((), ())), preferred_element_type=F32
        )

    copies[IMG_R0].wait_recv()
    same(FWD_R, im, part(zl, 0), right)

    copies[IMG_L1].wait_recv()
    same(FWD_L, im, part(zr, 1), left)
    for h, k in enumerate((TXT_X0, TXT_X1)):
        copies[k].wait_recv()

        @pl.when(jnp.logical_not(turn))
        def _():
            fwd[h].start()

        @pl.when(turn)
        def _():
            if h == 0:
                for copy in own + fwd:
                    copy.start()

    n_chunks = rows // CHUNK
    n_lane = tile // LANES
    lanes = lambda k: pl.ds(k * LANES, LANES)

    def stats_pair(q, p, order):
        first = p * 2 * rows

        def lane(k):
            return pl.ds(pl.multiple_of(first + k * LANES, LANES), LANES)

        @pl.loop(0, n_chunks, unroll=4)
        def _(r):
            where = pl.ds(pl.multiple_of(q * rows + r * CHUNK, CHUNK), CHUNK)
            parts = [s_ref[where, lane(k)] for k in range(n_lane // 2)]
            top = functools.reduce(jnp.maximum, parts)
            rowp[p, where, :] = top
            rows_s[p, where, :] = functools.reduce(jnp.add, [jnp.exp(v - top) for v in parts])

        @pl.loop(0, n_lane // 2)
        def _(k):
            span = lane(k)
            parts = [s_ref[pl.ds(pl.multiple_of(q * rows + 8 * r, 8), 8), span] for r in range(rows // 8)]
            top = functools.reduce(jnp.maximum, parts)
            at = pl.ds(pl.multiple_of(order * 8, 8), 8)
            colm[at, span] = top
            cols[at, span] = functools.reduce(jnp.add, [jnp.exp(v - top) for v in parts])

    def row_stats(q):
        top = jnp.maximum(rowp[0, block(q), :], rowp[1, block(q), :])
        total = functools.reduce(
            jnp.add, [rows_s[p, block(q), :] * jnp.exp(rowp[p, block(q), :] - top) for p in range(2)]
        )
        top = jnp.transpose(top)
        best = jnp.max(top, axis=0, keepdims=True)
        total = jnp.sum(jnp.transpose(total) * jnp.exp(top - best), axis=0, keepdims=True)
        rstat[:, block(q)] = jnp.broadcast_to(best + jnp.log(total), (8, rows))

    copies[IMG_R1].wait_recv()
    copies[IMG_L0].wait_recv()

    @pl.loop(0, 3)
    def _(t):
        logits_pair(pick(t, z, zl, zr), 0)
        stats_pair(pick(t, z, zl, zr), 0, t)

    for k in (TXT_N0, TXT_N1, FWD_N0, FWD_N1):
        copies[k].wait_recv()

    @pl.loop(0, 3)
    def _(t):
        logits_pair(pick(t, z, zl, zr), 1)
        stats_pair(pick(t, z, zl, zr), 1, t)
        row_stats(pick(t, z, zl, zr))

    copies[FWD_R].wait_recv()
    copies[FWD_L].wait_recv()

    @pl.loop(0, 2)
    def _(p):
        logits_pair(zf, p)
        stats_pair(zf, p, 3)

    row_stats(zf)

    def join(a, c):
        top = jnp.maximum(a, c)
        return top + jnp.log(jnp.exp(a - top) + jnp.exp(c - top))

    rstat[:, block(z)] = join(rstat[:, block(z)], jnp.broadcast_to(rr_ref[...].reshape(1, rows), (8, rows)))
    rl[z] = rstat[...]
    for k, target in ((ROW_R, right), (ROW_L, left), (ROW_F, far)):
        send(k, rstat, rl.at[z], target)
    top = jnp.max(colm[...], axis=0, keepdims=True)
    total = jnp.sum(cols[...] * jnp.exp(colm[...] - top), axis=0, keepdims=True)
    both = jnp.broadcast_to(top + jnp.log(total), (8, tile))
    co[i] = both[:, : 2 * rows]
    cp[2 + i] = both[:, 2 * rows :]
    co[i, :, block(i)] = join(co[i, :, block(i)], jnp.broadcast_to(rc_ref[...].reshape(1, rows), (8, rows)))
    send(OWN_X, co.at[i], co.at[i], across)
    send(OWN_NS, co.at[i], cp.at[i], n_same)
    send(OWN_NO, co.at[i], cp.at[i], n_other)
    send(PRV_X, cp.at[2 + i], cp.at[2 + i], across)
    send(PRV_PS, cp.at[2 + i], co.at[2 + i], p_same)
    send(PRV_PO, cp.at[2 + i], co.at[2 + i], p_other)

    def diag_pass(r, total):
        s = s_ref[pl.ds(pl.multiple_of(z * rows + r * CHUNK, CHUNK), CHUNK), block(i)]
        row = lax.broadcasted_iota(jnp.int32, s.shape, 0) + r * CHUNK
        return total + jnp.where(lax.broadcasted_iota(jnp.int32, s.shape, 1) == row, s, 0.0)

    diag = jnp.sum(lax.fori_loop(0, n_chunks, diag_pass, jnp.zeros((CHUNK, rows), F32)), keepdims=True)

    def merged(parts):
        top = functools.reduce(jnp.maximum, parts)
        return top + jnp.log(functools.reduce(jnp.add, [jnp.exp(p - top) for p in parts]))

    for k in range(ROW_R, PRV_PO + 1):
        copies[k].wait_recv()
    cl[:, : 2 * rows] = merged([co[k] for k in range(4)])
    cl[:, 2 * rows :] = merged([cp[k] for k in range(4)])
    rstat2 = merged([rl[k] for k in range(4)])
    for q in range(4):
        column = jnp.broadcast_to(rstat2[0:1, q * rows : (q + 1) * rows], (LANES, rows))
        rowp[0, pl.ds(q * rows, rows), :] = jnp.transpose(column)

    terms = (
        jnp.sum(rowp[0, block(z), 0:1], keepdims=True)
        + jnp.sum(cl[0:1, block(i)], keepdims=True)
        - 2.0 * diag
    )
    lacc[...] = jnp.broadcast_to(terms, lacc.shape)
    stages = [(z, [right, left, far]), (i, [across])]
    for step, count in blk_stages:
        stages.append(((b // step) % count, [dev(flips(b, step, k), i, z) for k in range(1, count)]))
    first_message = [SUM + sum(len(t) for _, t in stages[:k]) for k in range(len(stages))]

    def loss_send(k):
        place, targets = stages[k]
        terms_ref[k, place] = lacc[...]
        lsnd[k] = lacc[...]
        for j, target in enumerate(targets):
            send(first_message[k] + j, lsnd.at[k], terms_ref.at[k, place], target)

    def loss_next(k):
        targets = stages[k][1]
        for j in range(len(targets)):
            copies[first_message[k] + j].wait_recv()
        lacc[...] = functools.reduce(jnp.add, [terms_ref[k, j] for j in range(len(targets) + 1)])

    def weights_block(q):
        mine = q == z

        @pl.loop(0, n_chunks)
        def _(r):
            where = pl.ds(pl.multiple_of(q * rows + r * CHUNK, CHUNK), CHUNK)
            row_lse = rowp[0, where, :]
            row = lax.broadcasted_iota(jnp.int32, (CHUNK, LANES), 0) + (r * CHUNK + i * rows)
            target = jnp.where(mine, row, -1) - lax.broadcasted_iota(jnp.int32, (CHUNK, LANES), 1)
            for k in range(n_lane):
                s = s_ref[where, lanes(k)]
                value = jnp.exp(s - row_lse) + jnp.exp(s - cl[0:1, lanes(k)])
                if k < n_lane // 2:
                    value = value - jnp.where(target == k * LANES, 2.0, 0.0)
                w[where, lanes(k)] = value.astype(BF16)

    def image_product(q, h):
        return logit_scale * jnp.dot(w[part(q, h), :], tx[...], preferred_element_type=F32)

    def text_product(t):
        return logit_scale * lax.dot_general(
            w[:, block(t)], im[...], (((0,), (0,)), ((), ())), preferred_element_type=F32
        )

    def encode(value, unit, span):
        top = jnp.maximum(jnp.max(jnp.abs(value), axis=0, keepdims=True), 1e-30)
        snd[unit, pl.ds(half, PAD), span] = jnp.broadcast_to(top, (PAD, WIDE)).astype(BF16)
        top = snd[unit, pl.ds(half, PAD), span].astype(F32)[0:1]
        u = value * (POWER_RANGE / top)
        u2 = u * u
        u4 = u2 * u2
        snd[unit, pl.ds(0, half), span] = (u4 * u2 * u).astype(BF16)

    def decode(unit, span):
        code = rcv[unit, pl.ds(0, half), span].astype(F32)
        top = rcv[unit, pl.ds(half, PAD), span].astype(F32)[0:1] * (1.0 / POWER_RANGE)
        size = jnp.abs(code)
        root = jnp.exp2(jnp.log2(size) * (1.0 / 7.0))
        return jnp.where(size > 0.0, jnp.where(code < 0.0, -root, root), 0.0) * top

    def unit_send(unit, target):
        send(OUT + unit, snd.at[unit], rcv.at[unit], target)

    def arrived(unit):
        copies[OUT + unit].wait_recv()

    def columns(body):
        @pl.loop(0, width // WIDE)
        def _(n):
            body(pl.ds(pl.multiple_of(n * WIDE, WIDE), WIDE))

    lo, hi = pl.ds(0, half), pl.ds(half, half)

    def encode_all(ref, where, unit):
        @columns
        def _(span):
            encode(ref[where, span], unit, span)

    loss_send(0)
    weights_block(zf)
    loss_next(0)
    loss_send(1)

    @pl.loop(0, 2)
    def _(u):
        acc[lo, :] = image_product(zf, u)
        encode_all(acc, lo, u)
        remote(OUT + u, snd.at[u], rcv.at[u], dev(b, i, pick(u, zr, zl))).start()

    loss_next(1)
    loss_send(2)

    @pl.loop(0, 3)
    def _(t):
        weights_block(pick(t, zr, zl, z))

    loss_next(2)
    loss_send(3)
    back_turn = b % 8 == 0
    y_first = dev(prv, jnp.where(back_turn, oi, i), z)

    @pl.loop(0, 3)
    def _(t):
        acc[...] = text_product(pick(t, 2 + oi, 2 + i, oi))

        @pl.when(t < 2)
        def _():
            target = dev(prv, pick(t, jnp.where(back_turn, oi, i), i), z)
            for h, where in enumerate((lo, hi)):
                unit = Y_0 + 2 * t + h
                encode_all(acc, where, unit)
                remote(OUT + unit, snd.at[unit], rcv.at[unit], target).start()

    def relay(got, kept, where, out):
        arrived(got)

        @columns
        def _(span):
            encode(kept[where, span] + decode(got, span), out, span)

    for unit, target in ((Y_0, y_first), (Y_1, y_first), (Y_2, p_same), (Y_3, p_same)):
        copies[OUT + unit] = remote(OUT + unit, snd.at[unit], rcv.at[unit], target)
    for unit in (X_0, X_1):
        copies[OUT + unit] = remote(OUT + unit, snd.at[unit], rcv.at[unit], across)

    def relay_text():
        for got, where, out in ((Y_0, lo, X_0), (Y_1, hi, X_1)):
            relay(got, acc, where, out)
            copies[OUT + out].start()

    @pl.when(jnp.logical_not(odd))
    def _():
        relay_text()

    @pl.when(turn)
    def _():
        for where, out in ((lo, X_0), (hi, X_1)):
            encode_all(acc, where, out)
            copies[OUT + out].start()

    @pl.loop(0, 4)
    def _(u):
        value = image_product(pick(u, zr, zl, zr, zl), pick(u, 1, 0, 0, 1))
        keep[pick(u, 2, 2, 0, 1)] = value

        @pl.when(u < 2)
        def _():
            encode_all(keep.at[2], slice(None), R_DIR + u)
            remote(
                OUT + R_DIR + u, snd.at[R_DIR + u], rcv.at[R_DIR + u], dev(b, i, pick(u, zr, zl))
            ).start()

    for unit, target in (
        (F_R, right), (F_L, left), (R_DIR, right), (L_DIR, left)
    ):
        copies[OUT + unit] = remote(OUT + unit, snd.at[unit], rcv.at[unit], target)

    @pl.when(jnp.logical_and(odd, jnp.logical_not(turn)))
    def _():
        relay_text()

    relay(F_R, keep.at[0], lo, R_ACC)
    unit_send(R_ACC, right)
    relay(F_L, keep.at[1], lo, L_ACC)
    unit_send(L_ACC, left)

    tg_ref[...] = text_product(i)

    @pl.loop(0, 2)
    def _(h):
        ig_ref[pl.ds(pl.multiple_of(h * half, half), half), :] = image_product(z, h)

    loss_next(3)
    loss_ref[...] = lacc[0:1, 0:1] / (2.0 * (n_blk * 8 * rows))

    def add(got, ref, where):
        arrived(got)

        @columns
        def _(span):
            ref[where, span] = ref[where, span] + decode(got, span)

    @pl.when(turn)
    def _():
        for got, where in ((Y_0, lo), (Y_1, hi)):
            add(got, tg_ref, where)

    add(Y_2, tg_ref, lo)
    add(Y_3, tg_ref, hi)
    add(R_DIR, ig_ref, hi)
    add(L_DIR, ig_ref, lo)
    add(R_ACC, ig_ref, lo)
    add(L_ACC, ig_ref, hi)
    add(X_0, tg_ref, lo)
    add(X_1, tg_ref, hi)

    for copy in copies.values():
        copy.wait_send()


def shards(n_blk, images, texts, rest_row, rest_col):
    rows, width = images.shape
    tile = 4 * rows
    n_stage, n_sum = 4, 3 + 1 + 3 + 3
    vmem = pl.BlockSpec(memory_space=pltpu.VMEM)
    hbm = pl.BlockSpec(memory_space=pl.ANY)
    image_grad, text_grad, loss = pl.pallas_call(
        functools.partial(kernel, n_blk),
        out_shape=(
            jax.ShapeDtypeStruct((rows, width), F32),
            jax.ShapeDtypeStruct((rows, width), F32),
            jax.ShapeDtypeStruct((1, 1), F32),
        ),
        in_specs=[hbm, hbm, vmem, vmem],
        out_specs=(vmem, vmem, vmem),
        scratch_shapes=[
            pltpu.VMEM((tile, width), BF16),
            pltpu.VMEM((tile, width), BF16),
            pltpu.VMEM((tile, tile), F32),
            pltpu.VMEM((tile, tile), BF16),
            pltpu.VMEM((2, tile, LANES), F32),
            pltpu.VMEM((2, tile, LANES), F32),
            pltpu.VMEM((32, tile), F32),
            pltpu.VMEM((32, tile), F32),
            pltpu.VMEM((8, tile), F32),
            pltpu.VMEM((4, 8, tile), F32),
            pltpu.VMEM((4, 8, 2 * rows), F32),
            pltpu.VMEM((4, 8, 2 * rows), F32),
            pltpu.VMEM((8, tile), F32),
            pltpu.VMEM((3, rows // 2, width), F32),
            pltpu.VMEM((rows, width), F32),
            pltpu.VMEM((UNITS, rows // 2 + PAD, width), BF16),
            pltpu.VMEM((UNITS, rows // 2 + PAD, width), BF16),
            pltpu.VMEM((8, LANES), F32),
            pltpu.VMEM((n_stage, 8, LANES), F32),
            pltpu.VMEM((n_stage, 4, 8, LANES), F32),
            pltpu.SemaphoreType.DMA((SUM + n_sum,)),
            pltpu.SemaphoreType.DMA((SUM + n_sum,)),
            pltpu.SemaphoreType.DMA((2,)),
        ],
        compiler_params=pltpu.CompilerParams(
            collective_id=0, has_side_effects=True, vmem_limit_bytes=60 << 20
        ),
        cost_estimate=pl.CostEstimate(
            flops=6 * tile * tile * width, bytes_accessed=8 * rows * width * 4, transcendentals=4 * tile * tile
        ),
    )(images, texts, rest_row, rest_col)
    return image_grad, text_grad, loss.reshape(())


def solution(mesh):
    return jax.shard_map(
        functools.partial(shards, mesh.shape["blk"]),
        mesh=mesh,
        in_specs=(
            P(("blk", "node"), None),
            P(("blk", "node"), None),
            P(("blk", "node")),
            P(("blk", "node")),
        ),
        out_specs=(P(("blk", "node"), None), P(("blk", "node"), None), P()),
        check_vma=False,
    )
```

time: 165 us -> 135 us (0.82)
  the two profiles are of different devices: /device:TPU:2 before, /device:TPU:0 now
where the time goes in v2:
time: 135 us
  Pallas kernels  128 us (95%)
  local copies, waits for them, and re-layouts  4.36 us (3%)
  between operations  2.41 us (2%)
    pallas_call x1, Pallas kernels, shards(): pl.pallas_call(functools.partial(kernel, n_blk), out_shape=(jax.ShapeDtyp...  128 us
    unnamed x4, local copies, waits for them, and re-layouts  4.36 us

profile of v2, /device:TPU:0, one launch (start us, length us, event | category | flops | bytes accessed | tf_op | source)
XLA Modules:
  0.0 135.1 jit_solution(2659717666440781888)
XLA Ops:
  0.6 128.4 %shard_map.67 = (f32[384,1280]{1,0:T(8,128)}, f32[384,1280]{1,0:T(8,128)}, f32[1,1]{1,0:T(1,128)}) custom-call(bf16[384,1280]{1,0:T(8,128)(2,1)} %img_ref.1, bf16[384,1280]{1,0:T(8,128)(2,1)} %txt_ref.1, f32[384]{0:T(512)} %rr_ref.1, f32[384]{0:T(512)} %rc_ref.1), custom_call_target="tpu_custom_call" | custom-call | flops 18119393280 | bytes 15728640 | tf_op jit(solution)/shard_map/pallas_call | solution.py:475
  129.0 0.0 copy-start
  129.0 3.1 %copy.10 = f32[384,1280]{1,0:T(8,128)} copy(f32[384,1280]{1,0:T(8,128)} %get-tuple-element.12) | data formatting | bytes 3932160
  132.1 0.0 copy-done
  132.1 1.3 copy.11
Async XLA Ops:
  129.0 3.1 %copy-start = (f32[384,1280]{1,0:T(8,128)S(1)}, f32[384,1280]{1,0:T(8,128)}, u32[]{:S(2)}) copy-start(f32[384,1280]{1,0:T(8,128)} %get-tuple-element.13) | copy-start | bytes 5898244

commit v3 on v2

--- a/solution.py
+++ b/solution.py
@@ -19,7 +19,8 @@
 
 (IMG_R0, IMG_R1, IMG_L1, IMG_L0, FWD_R, FWD_L, TXT_X0, TXT_X1, TXT_N0, TXT_N1, FWD_N0, FWD_N1) = range(12)
 (ROW_R, ROW_L, ROW_F, OWN_X, OWN_NS, OWN_NO, PRV_X, PRV_PS, PRV_PO) = range(12, 21)
-OUT = 21
+(VIA_0, VIA_1, VIA_S0, VIA_S1, VIA_O0, VIA_O1) = range(21, 27)
+OUT = 27
 (F_R, F_L, R_DIR, L_DIR, R_ACC, L_ACC, Y_0, Y_1, Y_2, Y_3, X_0, X_1) = range(12)
 UNITS = 12
 SUM = OUT + UNITS
@@ -27,7 +28,7 @@
 
 def kernel(
     n_blk, img_ref, txt_ref, rr_ref, rc_ref, ig_ref, tg_ref, loss_ref,
-    im, tx, s_ref, w, rowp, rows_s, colm, cols, rstat, rl, co, cp, cl, keep, acc, snd, rcv, lacc, lsnd, terms_ref,
+    im, tx, s_ref, w, rowp, rows_s, colm, cols, rstat, rl, co, cp, cl, keep, acc, via, snd, rcv, lacc, lsnd, terms_ref,
     ss, rs, lsem,
 ):
     rows, width = img_ref.shape
@@ -72,7 +73,23 @@
         partners += [dev(flips(b, step, k), i, z) for k in range(1, count) if step * k != 1]
     for partner in partners:
         pl.semaphore_signal(barrier, inc=1, device_id=partner, device_id_type=MESH)
-    pl.semaphore_wait(barrier, len(partners))
+
+    turn, between, ahead = b % 8 == 7, b % 8 == 1, b % 8 == 0
+    via_dev = dev((b + n_blk - 6) % n_blk, i, z)
+    via_from = dev((b + 6) % n_blk, i, z)
+    via_same, via_other = dev((b + 7) % n_blk, i, z), dev((b + 7) % n_blk, oi, z)
+    from_same, from_other = dev((b + n_blk - 7) % n_blk, i, z), dev((b + n_blk - 7) % n_blk, oi, z)
+    for role, others in (
+        (turn, [via_dev]), (between, [via_from, via_same, via_other]), (ahead, [from_same, from_other])
+    ):
+
+        @pl.when(role)
+        def _():
+            for partner in others:
+                pl.semaphore_signal(barrier, inc=1, device_id=partner, device_id_type=MESH)
+
+    extra = jnp.where(turn, 1, 0) + jnp.where(between, 3, 0) + jnp.where(ahead, 2, 0)
+    pl.semaphore_wait(barrier, len(partners) + extra)
     load_img.wait()
     load_txt.wait()
 
@@ -97,7 +114,6 @@
         send(k, ref.at[where], ref.at[where], target)
 
     odd = b % 2 == 1
-    turn = b % 8 == 7
 
     def start(k, src, dst, target):
         copies[k] = remote(k, src, dst, target)
@@ -109,6 +125,27 @@
         start(k, tx.at[part(i, h)], tx.at[part(2 + i, h)], n_same) for h, k in enumerate((TXT_N0, TXT_N1))
     ]
 
+    via_in = [start(k, tx.at[part(i, h)], via.at[pl.ds(h * half, half)], via_dev) for h, k in enumerate((VIA_0, VIA_1))]
+    via_out = [
+        pltpu.make_async_remote_copy(
+            src_ref=via.at[pl.ds(h * half, half)],
+            dst_ref=tx.at[part(2 + i, h)],
+            send_sem=ss.at[k],
+            recv_sem=rs.at[landing],
+            device_id=target,
+            device_id_type=MESH,
+        )
+        for h, k, landing, target in (
+            (0, VIA_S0, TXT_N0, via_same), (0, VIA_O0, FWD_N0, via_other),
+            (1, VIA_S1, TXT_N1, via_same), (1, VIA_O1, FWD_N1, via_other),
+        )
+    ]
+
+    @pl.when(turn)
+    def _():
+        via_in[0].start()
+        via_in[1].start()
+
     @pl.when(jnp.logical_not(turn))
     def _():
         own[0].start()
@@ -121,10 +158,8 @@
 
     same(IMG_R1, im, part(z, 1), right)
     same(IMG_L0, im, part(z, 0), left)
-    slot = jnp.where(turn, i, oi)
-    reach = dev(nxt, jnp.where(turn, oi, i), z)
     fwd = [
-        start(k, tx.at[part(slot, h)], tx.at[part(2 + slot, h)], reach) for h, k in enumerate((FWD_N0, FWD_N1))
+        start(k, tx.at[part(oi, h)], tx.at[part(2 + oi, h)], n_same) for h, k in enumerate((FWD_N0, FWD_N1))
     ]
 
     def pick(t, *options):
@@ -139,6 +174,13 @@
             im[block(q), :], tx[pair, :], (((1,), (1,)), ((), ())), preferred_element_type=F32
         )
 
+    @pl.when(between)
+    def _():
+        for h in range(2):
+            via_in[h].wait_recv()
+            via_out[2 * h].start()
+            via_out[2 * h + 1].start()
+
     copies[IMG_R0].wait_recv()
     same(FWD_R, im, part(zl, 0), right)
 
@@ -150,12 +192,6 @@
         @pl.when(jnp.logical_not(turn))
         def _():
             fwd[h].start()
-
-        @pl.when(turn)
-        def _():
-            if h == 0:
-                for copy in own + fwd:
-                    copy.start()
 
     n_chunks = rows // CHUNK
     n_lane = tile // LANES
@@ -362,22 +398,8 @@
     def _(t):
         weights_block(pick(t, zr, zl, z))
 
-    loss_next(2)
-    loss_send(3)
     back_turn = b % 8 == 0
     y_first = dev(prv, jnp.where(back_turn, oi, i), z)
-
-    @pl.loop(0, 3)
-    def _(t):
-        acc[...] = text_product(pick(t, 2 + oi, 2 + i, oi))
-
-        @pl.when(t < 2)
-        def _():
-            target = dev(prv, pick(t, jnp.where(back_turn, oi, i), i), z)
-            for h, where in enumerate((lo, hi)):
-                unit = Y_0 + 2 * t + h
-                encode_all(acc, where, unit)
-                remote(OUT + unit, snd.at[unit], rcv.at[unit], target).start()
 
     def relay(got, kept, where, out):
         arrived(got)
@@ -396,7 +418,25 @@
             relay(got, acc, where, out)
             copies[OUT + out].start()
 
-    @pl.when(jnp.logical_not(odd))
+    @pl.loop(0, 3)
+    def _(t):
+        slot = jnp.where(back_turn, pick(t, oi, 2 + oi, 2 + i), pick(t, 2 + oi, 2 + i, oi))
+        acc[...] = text_product(slot)
+
+        @pl.when(jnp.logical_and(back_turn, t == 0))
+        def _():
+            relay_text()
+
+        @pl.when(slot >= 2)
+        def _():
+            turned = t - jnp.where(back_turn, 1, 0)
+            target = dev(prv, pick(turned, jnp.where(back_turn, oi, i), i), z)
+            for h, where in enumerate((lo, hi)):
+                unit = Y_0 + 2 * turned + h
+                encode_all(acc, where, unit)
+                remote(OUT + unit, snd.at[unit], rcv.at[unit], target).start()
+
+    @pl.when(jnp.logical_not(jnp.logical_or(odd, back_turn)))
     def _():
         relay_text()
 
@@ -427,6 +467,8 @@
     def _():
         relay_text()
 
+    loss_next(2)
+    loss_send(3)
     relay(F_R, keep.at[0], lo, R_ACC)
     unit_send(R_ACC, right)
     relay(F_L, keep.at[1], lo, L_ACC)
@@ -462,8 +504,15 @@
     add(X_0, tg_ref, lo)
     add(X_1, tg_ref, hi)
 
-    for copy in copies.values():
-        copy.wait_send()
+    for k, copy in copies.items():
+        if k not in (TXT_N0, TXT_N1, FWD_N0, FWD_N1, VIA_0, VIA_1):
+            copy.wait_send()
+    for role, sent in ((turn, via_in), (between, via_out), (jnp.logical_not(turn), own + fwd)):
+
+        @pl.when(role)
+        def _():
+            for copy in sent:
+                copy.wait_send()
 
 
 def shards(n_blk, images, texts, rest_row, rest_col):
@@ -497,6 +546,7 @@
             pltpu.VMEM((8, tile), F32),
             pltpu.VMEM((3, rows // 2, width), F32),
             pltpu.VMEM((rows, width), F32),
+            pltpu.VMEM((rows, width), BF16),
             pltpu.VMEM((UNITS, rows // 2 + PAD, width), BF16),
             pltpu.VMEM((UNITS, rows // 2 + PAD, width), BF16),
             pltpu.VMEM((8, LANES), F32),

time: 135 us -> 124 us (0.919)
  the two profiles are of different devices: /device:TPU:0 before, /device:TPU:25 now
where the time goes in v3:
time: 124 us
  Pallas kernels  117 us (94%)
  local copies, waits for them, and re-layouts  4.36 us (4%)
  between operations  2.41 us (2%)
    pallas_call x1, Pallas kernels, shards(): pl.pallas_call(functools.partial(kernel, n_blk), out_shape=(jax.ShapeDtyp...  117 us
    unnamed x4, local copies, waits for them, and re-layouts  4.36 us

profile of v3, /device:TPU:25, one launch (start us, length us, event | category | flops | bytes accessed | tf_op | source)
XLA Modules:
  0.0 124.1 jit_solution(16211013396625434134)
XLA Ops:
  0.6 117.3 %shard_map.67 = (f32[384,1280]{1,0:T(8,128)}, f32[384,1280]{1,0:T(8,128)}, f32[1,1]{1,0:T(1,128)}) custom-call(bf16[384,1280]{1,0:T(8,128)(2,1)} %img_ref.1, bf16[384,1280]{1,0:T(8,128)(2,1)} %txt_ref.1, f32[384]{0:T(512)} %rr_ref.1, f32[384]{0:T(512)} %rc_ref.1), custom_call_target="tpu_custom_call" | custom-call | flops 18119393280 | bytes 15728640 | tf_op jit(solution)/shard_map/pallas_call | solution.py:524
  118.0 0.0 copy-start
  118.0 3.1 %copy.10 = f32[384,1280]{1,0:T(8,128)} copy(f32[384,1280]{1,0:T(8,128)} %get-tuple-element.12) | data formatting | bytes 3932160
  121.1 0.0 copy-done
  121.1 1.3 %copy.11 = f32[384,1280]{1,0:T(8,128)} copy(f32[384,1280]{1,0:T(8,128)S(1)} %copy-done) | data formatting | bytes 3932160
Async XLA Ops:
  118.0 3.1 %copy-start = (f32[384,1280]{1,0:T(8,128)S(1)}, f32[384,1280]{1,0:T(8,128)}, u32[]{:S(2)}) copy-start(f32[384,1280]{1,0:T(8,128)} %get-tuple-element.13) | copy-start | bytes 5898244

commit v4 on v3

--- a/solution.py
+++ b/solution.py
@@ -20,7 +20,8 @@
 (IMG_R0, IMG_R1, IMG_L1, IMG_L0, FWD_R, FWD_L, TXT_X0, TXT_X1, TXT_N0, TXT_N1, FWD_N0, FWD_N1) = range(12)
 (ROW_R, ROW_L, ROW_F, OWN_X, OWN_NS, OWN_NO, PRV_X, PRV_PS, PRV_PO) = range(12, 21)
 (VIA_0, VIA_1, VIA_S0, VIA_S1, VIA_O0, VIA_O1) = range(21, 27)
-OUT = 27
+(BACK_0, BACK_1) = range(27, 29)
+OUT = 29
 (F_R, F_L, R_DIR, L_DIR, R_ACC, L_ACC, Y_0, Y_1, Y_2, Y_3, X_0, X_1) = range(12)
 UNITS = 12
 SUM = OUT + UNITS
@@ -28,7 +29,7 @@
 
 def kernel(
     n_blk, img_ref, txt_ref, rr_ref, rc_ref, ig_ref, tg_ref, loss_ref,
-    im, tx, s_ref, w, rowp, rows_s, colm, cols, rstat, rl, co, cp, cl, keep, acc, via, snd, rcv, lacc, lsnd, terms_ref,
+    im, tx, s_ref, w, rowp, rows_s, colm, cols, rstat, rl, co, cp, cl, keep, acc, via, bk, snd, rcv, lacc, lsnd, terms_ref,
     ss, rs, lsem,
 ):
     rows, width = img_ref.shape
@@ -79,8 +80,14 @@
     via_from = dev((b + 6) % n_blk, i, z)
     via_same, via_other = dev((b + 7) % n_blk, i, z), dev((b + 7) % n_blk, oi, z)
     from_same, from_other = dev((b + n_blk - 7) % n_blk, i, z), dev((b + n_blk - 7) % n_blk, oi, z)
+    backer = b % 8 == 6
+    back_dev, back_src = dev((b + 6) % n_blk, i, z), dev((b + 7) % n_blk, i, z)
+    back_from, back_to = dev((b + n_blk - 6) % n_blk, i, z), dev((b + n_blk - 7) % n_blk, i, z)
     for role, others in (
-        (turn, [via_dev]), (between, [via_from, via_same, via_other]), (ahead, [from_same, from_other])
+        (turn, [via_dev, back_src]),
+        (between, [via_from, via_same, via_other]),
+        (ahead, [from_same, from_other, back_dev]),
+        (backer, [back_from, back_to]),
     ):
 
         @pl.when(role)
@@ -88,7 +95,7 @@
             for partner in others:
                 pl.semaphore_signal(barrier, inc=1, device_id=partner, device_id_type=MESH)
 
-    extra = jnp.where(turn, 1, 0) + jnp.where(between, 3, 0) + jnp.where(ahead, 2, 0)
+    extra = jnp.where(turn, 2, 0) + jnp.where(between, 3, 0) + jnp.where(ahead, 3, 0) + jnp.where(backer, 2, 0)
     pl.semaphore_wait(barrier, len(partners) + extra)
     load_img.wait()
     load_txt.wait()
@@ -434,7 +441,22 @@
             for h, where in enumerate((lo, hi)):
                 unit = Y_0 + 2 * turned + h
                 encode_all(acc, where, unit)
-                remote(OUT + unit, snd.at[unit], rcv.at[unit], target).start()
+                passed_on = jnp.logical_and(back_turn, turned == 1)
+
+                @pl.when(jnp.logical_not(passed_on))
+                def _():
+                    remote(OUT + unit, snd.at[unit], rcv.at[unit], target).start()
+
+                @pl.when(passed_on)
+                def _():
+                    pltpu.make_async_remote_copy(
+                        src_ref=snd.at[unit],
+                        dst_ref=bk.at[h],
+                        send_sem=ss.at[OUT + unit],
+                        recv_sem=rs.at[BACK_0 + h],
+                        device_id=back_dev,
+                        device_id_type=MESH,
+                    ).start()
 
     @pl.when(jnp.logical_not(jnp.logical_or(odd, back_turn)))
     def _():
@@ -473,6 +495,25 @@
     unit_send(R_ACC, right)
     relay(F_L, keep.at[1], lo, L_ACC)
     unit_send(L_ACC, left)
+    back_in = [remote(BACK_0 + h, bk.at[h], bk.at[h], back_dev) for h in range(2)]
+    back_out = [
+        pltpu.make_async_remote_copy(
+            src_ref=bk.at[h],
+            dst_ref=rcv.at[Y_2 + h],
+            send_sem=ss.at[BACK_0 + h],
+            recv_sem=rs.at[OUT + Y_2 + h],
+            device_id=back_to,
+            device_id_type=MESH,
+        )
+        for h in range(2)
+    ]
+
+    @pl.when(backer)
+    def _():
+        for h in range(2):
+            back_in[h].wait_recv()
+            back_out[h].start()
+
 
     tg_ref[...] = text_product(i)
 
@@ -507,7 +548,9 @@
     for k, copy in copies.items():
         if k not in (TXT_N0, TXT_N1, FWD_N0, FWD_N1, VIA_0, VIA_1):
             copy.wait_send()
-    for role, sent in ((turn, via_in), (between, via_out), (jnp.logical_not(turn), own + fwd)):
+    for role, sent in (
+        (turn, via_in), (between, via_out), (jnp.logical_not(turn), own + fwd), (backer, back_out)
+    ):
 
         @pl.when(role)
         def _():
@@ -547,6 +590,7 @@
             pltpu.VMEM((3, rows // 2, width), F32),
             pltpu.VMEM((rows, width), F32),
             pltpu.VMEM((rows, width), BF16),
+            pltpu.VMEM((2, rows // 2 + PAD, width), BF16),
             pltpu.VMEM((UNITS, rows // 2 + PAD, width), BF16),
             pltpu.VMEM((UNITS, rows // 2 + PAD, width), BF16),
             pltpu.VMEM((8, LANES), F32),

time: 124 us -> 121 us (0.976)
  Pallas kernels: 117 us -> 114 us
    pallas_call x1, Pallas kernels: 117 us -> 114 us  [shards(): pl.pallas_call(functools.partial(kernel, n_blk), out_shape=(jax.ShapeDtyp...]
where the time goes in v4:
time: 121 us
  Pallas kernels  114 us (94%)
  local copies, waits for them, and re-layouts  4.36 us (4%)
  between operations  2.41 us (2%)
    pallas_call x1, Pallas kernels, shards(): pl.pallas_call(functools.partial(kernel, n_blk), out_shape=(jax.ShapeDtyp...  114 us
    unnamed x4, local copies, waits for them, and re-layouts  4.36 us

profile of v4, /device:TPU:25, one launch (start us, length us, event | category | flops | bytes accessed | tf_op | source)
XLA Modules:
  0.0 120.8 jit_solution(12805522411644070538)
XLA Ops:
  0.6 114.0 %shard_map.67 = (f32[384,1280]{1,0:T(8,128)}, f32[384,1280]{1,0:T(8,128)}, f32[1,1]{1,0:T(1,128)}) custom-call(bf16[384,1280]{1,0:T(8,128)(2,1)} %img_ref.1, bf16[384,1280]{1,0:T(8,128)(2,1)} %txt_ref.1, f32[384]{0:T(512)} %rr_ref.1, f32[384]{0:T(512)} %rc_ref.1), custom_call_target="tpu_custom_call" | custom-call | flops 18119393280 | bytes 15728640 | tf_op jit(solution)/shard_map/pallas_call | solution.py:567
  114.6 0.0 copy-start
  114.6 3.1 %copy.10 = f32[384,1280]{1,0:T(8,128)} copy(f32[384,1280]{1,0:T(8,128)} %get-tuple-element.12) | data formatting | bytes 3932160
  117.7 0.0 copy-done
  117.7 1.3 %copy.11 = f32[384,1280]{1,0:T(8,128)} copy(f32[384,1280]{1,0:T(8,128)S(1)} %copy-done) | data formatting | bytes 3932160
Async XLA Ops:
  114.6 3.1 %copy-start = (f32[384,1280]{1,0:T(8,128)S(1)}, f32[384,1280]{1,0:T(8,128)}, u32[]{:S(2)}) copy-start(f32[384,1280]{1,0:T(8,128)} %get-tuple-element.13) | copy-start | bytes 5898244

commit v5 on v4

--- a/solution.py
+++ b/solution.py
@@ -521,8 +521,6 @@
     def _(h):
         ig_ref[pl.ds(pl.multiple_of(h * half, half), half), :] = image_product(z, h)
 
-    loss_next(3)
-    loss_ref[...] = lacc[0:1, 0:1] / (2.0 * (n_blk * 8 * rows))
 
     def add(got, ref, where):
         arrived(got)
@@ -531,13 +529,14 @@
         def _(span):
             ref[where, span] = ref[where, span] + decode(got, span)
 
-    @pl.when(turn)
-    def _():
-        for got, where in ((Y_0, lo), (Y_1, hi)):
-            add(got, tg_ref, where)
-
-    add(Y_2, tg_ref, lo)
-    add(Y_3, tg_ref, hi)
+    def add_back():
+        add(Y_2, tg_ref, lo)
+        add(Y_3, tg_ref, hi)
+
+    @pl.when(jnp.logical_not(turn))
+    def _():
+        add_back()
+
     add(R_DIR, ig_ref, hi)
     add(L_DIR, ig_ref, lo)
     add(R_ACC, ig_ref, lo)
@@ -545,6 +544,14 @@
     add(X_0, tg_ref, lo)
     add(X_1, tg_ref, hi)
 
+    @pl.when(turn)
+    def _():
+        add_back()
+        for got, where in ((Y_0, lo), (Y_1, hi)):
+            add(got, tg_ref, where)
+
+    loss_next(3)
+    loss_ref[...] = lacc[0:1, 0:1] / (2.0 * (n_blk * 8 * rows))
     for k, copy in copies.items():
         if k not in (TXT_N0, TXT_N1, FWD_N0, FWD_N1, VIA_0, VIA_1):
             copy.wait_send()

time: 121 us -> 118 us (0.975)
  Pallas kernels: 114 us -> 111 us
    pallas_call x1, Pallas kernels: 114 us -> 111 us  [shards(): pl.pallas_call(functools.partial(kernel, n_blk), out_shape=(jax.ShapeDtyp...]
where the time goes in v5:
time: 118 us
  Pallas kernels  111 us (94%)
  local copies, waits for them, and re-layouts  4.36 us (4%)
  between operations  2.41 us (2%)
    pallas_call x1, Pallas kernels, shards(): pl.pallas_call(functools.partial(kernel, n_blk), out_shape=(jax.ShapeDtyp...  111 us
    unnamed x4, local copies, waits for them, and re-layouts  4.36 us

profile of v5, /device:TPU:25, one launch (start us, length us, event | category | flops | bytes accessed | tf_op | source)
XLA Modules:
  0.0 117.9 jit_solution(5837626306950147091)
XLA Ops:
  0.6 111.1 %shard_map.67 = (f32[384,1280]{1,0:T(8,128)}, f32[384,1280]{1,0:T(8,128)}, f32[1,1]{1,0:T(1,128)}) custom-call(bf16[384,1280]{1,0:T(8,128)(2,1)} %img_ref.1, bf16[384,1280]{1,0:T(8,128)(2,1)} %txt_ref.1, f32[384]{0:T(512)} %rr_ref.1, f32[384]{0:T(512)} %rc_ref.1), custom_call_target="tpu_custom_call" | custom-call | flops 18119393280 | bytes 15728640 | tf_op jit(solution)/shard_map/pallas_call | solution.py:574
  111.7 0.0 copy-start
  111.7 3.1 %copy.10 = f32[384,1280]{1,0:T(8,128)} copy(f32[384,1280]{1,0:T(8,128)} %get-tuple-element.12) | data formatting | bytes 3932160
  114.8 0.0 copy-done
  114.8 1.3 %copy.11 = f32[384,1280]{1,0:T(8,128)} copy(f32[384,1280]{1,0:T(8,128)S(1)} %copy-done) | data formatting | bytes 3932160
Async XLA Ops:
  111.7 3.1 %copy-start = (f32[384,1280]{1,0:T(8,128)S(1)}, f32[384,1280]{1,0:T(8,128)}, u32[]{:S(2)}) copy-start(f32[384,1280]{1,0:T(8,128)} %get-tuple-element.13) | copy-start | bytes 5898244
